TPU v7x, 256 devices: a whole 4x4x8 slice. The times are simulated.
256 devices in a mesh: prow: 16 (over x_lo, z), pcol: 16 (over x_hi, y, core).
Axes of the slice: x: 4 (x_hi: 2, x_lo: 2; x = x_hi * 2 + x_lo), y: 4, z: 8, core: 2. Of those that a mesh axis runs over, the one named last changes fastest.
Arguments:
- inverse_blocks: bfloat16 [3, 2, 16, 512, 2, 16, 512], P(None, None, 'prow', None, None, 'pcol'), may hold values from -0.375 to 0.375
- factor_cols: bfloat16 [3, 2, 16, 512, 512], P(None, None, 'prow', 'pcol'), may hold values from -0.23925781 to 0.23925781
- diag_inverse: float32 [3, 512, 512], replicated, may hold values from -6 to 6
- block_mask: int32 [3, 32, 32], replicated, may hold values 0 or 1
Outputs:
- inverse_cols: float32 [3, 2, 16, 512, 512], P(None, None, 'prow', 'pcol')
- inverse_diag: float32 [3, 512, 512], replicated
All inputs are finite; a program needn't handle non-finite values.
Results may differ from a plain program's by a relative error of at most 0.0003.
Values may be sent and summed in bfloat16 or wider, within the bound.
A program may use at most 128 MiB of HBM per device.

v0:
```python
import jax
import jax.numpy as jnp
from jax import lax
from jax.sharding import PartitionSpec as P


def spread(block, axis, source):
    block = jnp.where(lax.axis_index(axis) == source, block, jnp.zeros_like(block))
    return lax.psum(block, axis)


def shards(inverse_blocks, factor_cols, diag_inverse, block_mask):
    grid_rows = lax.axis_size("prow")
    grid_cols = lax.axis_size("pcol")
    row_index = lax.axis_index("prow")
    col_index = lax.axis_index("pcol")
    nodes, row_blocks, unused_a, block_size, col_blocks, unused_b, unused_c = inverse_blocks.shape
    width = factor_cols.shape[-1]
    row_group = lax.all_gather(factor_cols, "pcol", axis=3, tiled=True)
    arrived = spread(row_group, "prow", 0 * grid_cols + col_index)
    arrivals = [arrived[:, :, 0]]
    col_group = jnp.stack(arrivals, axis=2).reshape(nodes, col_blocks, block_size, width)
    masks = block_mask.reshape(nodes, row_blocks, grid_rows, col_blocks, grid_cols)
    owned_mask = lax.dynamic_index_in_dim(masks, row_index, 2, keepdims=False)
    owned_mask = lax.dynamic_index_in_dim(owned_mask, col_index, 3, keepdims=False)
    local = inverse_blocks.reshape(nodes, row_blocks, block_size, col_blocks, block_size)
    local = local * owned_mask[:, :, None, :, None].astype(jnp.bfloat16)
    highest = lax.Precision.HIGHEST
    term = -jnp.einsum("smaqb,sqbw->smaw", local, col_group, preferred_element_type=jnp.float32)
    columns = lax.psum_scatter(term, "pcol", scatter_dimension=2, tiled=True)
    owned_rows = factor_cols[:, :, 0].astype(jnp.float32)
    diag_term = lax.psum(
        jnp.einsum("smaw,smav->swv", owned_rows, columns, precision=highest), ("prow", "pcol")
    )
    inverse_cols = columns.reshape(nodes, row_blocks, 1, block_size // grid_cols, width)
    inverse_diag = diag_inverse - diag_term
    return (inverse_cols, inverse_diag)


def solution(mesh):
    placed = (
        P(None, None, "prow", None, None, "pcol", None),
        P(None, None, "prow", "pcol", None),
        P(),
        P(),
    )
    return jax.shard_map(
        shards,
        mesh=mesh,
        in_specs=placed,
        out_specs=(P(None, None, "prow", "pcol", None), P()),
        check_vma=False,
    )
```

profile of v0, /device:TPU:1, one launch (start us, length us, event | category | flops | bytes accessed | tf_op | source)
XLA Modules:
  0.0 607.1 jit_solution(16488150177668037660)
XLA Ops:
  7.2 0.0 all-gather.2.cloned.1.call-start
  7.2 0.7 all-gather.2.cloned.1.call-update
  7.9 0.0 all-reduce.3.cloned.1.call-start
  8.0 62.9 %all-gather.2.cloned.1.call-done = bf16[3,2,1,512,512]{4,3,1,0,2:T(8,128)(2,1)} async-done(((bf16[3,2,1,32,512]{4,3,1,0,2:T(8,128)(2,1)}), bf16[3,2,1,512,512]{4,3,1,0,2:T(8,128)(2,1)}) %all-gather.2.cloned.1.call-update) | async-done | bytes 3145744 | tf_op jit(solution)/shard_map/all_gather | solution.py:19
  70.8 1.9 select_bitcast_fusion
  72.7 0.0 copy-start.1
  72.7 0.0 all-reduce.3.cloned.1.call-update
  72.7 0.0 reduce-scatter.2.cloned.1.call-start
  72.8 0.7 copy-done.1
  73.5 0.1 reshape.19
  73.6 0.1 constant_dynamic-slice_fusion
  73.7 0.1 copy.16
  73.8 0.1 copy.7
  73.9 8.2 %bitcast_multiply_fusion = bf16[3,2,512,2,512]{4,3,2,1,0:T(2,128)(2,1)} fusion(bf16[3,2,1,512,2,1,512]{6,4,5,3,2,1,0:T(2,128)(2,1)} %param.4, bf16[3,2,2]{2,1,0:T(2,128)(2,1)S(1)} %copy.7), kind=kLoop, calls=%fused_computation.1 | loop fusion | flops 3145728 | bytes 12582936 | tf_op jit(solution)/shard_map/mul | solution.py:27
  82.2 128.4 %all-reduce.3.cloned.1.call-done = bf16[3,2,512,512]{3,2,1,0:T(8,128)(2,1)} async-done(((bf16[3,2,512,512]{3,2,1,0:T(8,128)(2,1)}), bf16[3,2,512,512]{3,2,1,0:T(8,128)(2,1)}) %all-reduce.3.cloned.1.call-update) | async-done | bytes 3145744 | tf_op jit(solution)/shard_map/psum | solution.py:9
  210.6 9.8 %bitcast_negate_fusion = f32[3,2,512,512]{3,2,1,0:T(8,128)} fusion(bf16[3,2,512,512]{3,2,1,0:T(8,128)(2,1)} %all-reduce.3.cloned.1.call-done, bf16[3,2,512,2,512]{4,3,2,1,0:T(2,128)(2,1)} %bitcast_multiply_fusion), kind=kOutput, calls=%fused_computation | convolution fusion | flops 3222798336 | bytes 15728640 | tf_op jit(solution)/shard_map/smaqb,sqbw->smaw/dot_general | solution.py:29
  220.4 0.0 copy-start
  220.4 0.0 reduce-scatter.2.cloned.1.call-update
  220.4 0.0 all-reduce.5.cloned.1.call-start
  220.4 102.5 %reduce-scatter.2.cloned.1.call-done = f32[3,2,32,512]{3,2,1,0:T(8,128)} async-done(((f32[3,2,512,512]{3,2,1,0:T(8,128)}), f32[3,2,32,512]{3,2,1,0:T(8,128)}) %reduce-scatter.2.cloned.1.call-update) | async-done | bytes 393232 | tf_op jit(solution)/shard_map/reduce_scatter | solution.py:30
  323.0 0.0 copy-done
  323.0 4.1 convolution_bitcast_fusion
  327.1 0.0 all-reduce.5.cloned.1.call-update
  327.1 2.4 copy.10
  329.5 263.2 %all-reduce.5.cloned.1.call-done = f32[3,512,512]{1,2,0:T(8,128)} async-done(((f32[3,512,512]{1,2,0:T(8,128)}), f32[3,512,512]{1,2,0:T(8,128)}) %all-reduce.5.cloned.1.call-update) | async-done | bytes 3145744 | tf_op jit(solution)/shard_map/psum | solution.py:32
  592.7 4.3 sub.3
  597.0 3.5 copy.12
  (1 shorter events, 0.0 us)
Async XLA Ops:
  7.2 63.7 %all-gather.2.cloned.1.call-start = ((), (), s32[]{:S(2)}) async-start(), calls=%async_computation.1 | async-start | bytes 3342336 | tf_op jit(solution)/shard_map/all_gather | solution.py:19
  7.9 202.7 %all-reduce.3.cloned.1.call-start = ((), (), s32[]{:S(2)}) async-start(), calls=%async_computation.2 | async-start | bytes 6291456 | tf_op jit(solution)/shard_map/psum | solution.py:9
  72.7 0.8 copy-start.1
  72.7 250.3 %reduce-scatter.2.cloned.1.call-start = ((), (), s32[]{:S(2)}) async-start(), calls=%async_computation.3 | async-start | bytes 6684672 | tf_op jit(solution)/shard_map/reduce_scatter | solution.py:30
  220.4 102.6 %copy-start = (bf16[3,2,1,32,512]{4,3,2,1,0:T(8,128)(2,1)S(1)}, bf16[3,2,1,32,512]{4,3,2,1,0:T(8,128)(2,1)}, u32[]{:S(2)}) copy-start(bf16[3,2,1,32,512]{4,3,2,1,0:T(8,128)(2,1)} %param.5) | copy-start | bytes 589828
  220.4 372.3 %all-reduce.5.cloned.1.call-start = ((), (), s32[]{:S(2)}) async-start(), calls=%async_computation.4 | async-start | bytes 6291456 | tf_op jit(solution)/shard_map/psum | solution.py:32
Sparse Core Ops, SparseCore 0:
  10.8 59.9 all-gather.1
  74.1 136.4 all-reduce.2
  220.5 102.4 reduce-scatter.1
  329.7 262.9 all-reduce.4
where the time goes:
time: 608 us; the launch traced here: 607 us
  waiting for transfers between devices  558 us (92%)
  other arithmetic  14.4 us (2%)
  matrix products  13.9 us (2%)
  between operations  13.8 us (2%)
  local copies, waits for them, and re-layouts  7.06 us (1%)
    psum x1, waiting for transfers between devices, shards(): lax.psum(jnp.einsum('smaw,smav->swv', owned_rows, columns, precision=high...  263 us
    psum x1, waiting for transfers between devices, spread(): return lax.psum(block, axis)  128 us
    reduce_scatter x1, waiting for transfers between devices, shards(): columns = lax.psum_scatter(term, 'pcol', scatter_dimension=2, tiled=True)  103 us
    all_gather x1, waiting for transfers between devices, shards(): row_group = lax.all_gather(factor_cols, 'pcol', axis=3, tiled=True)  62.9 us
  transfers between devices with their start and end apart: 4, of which 4 were waited for; matrix products, arithmetic and copies ran while one was open for 2% of the time, Pallas kernels for 0%

commit v1 on v0

v1 whole, which is shorter than its diff:
```python
import jax
import jax.numpy as jnp
from jax import lax
from jax.experimental import pallas as pl
from jax.experimental.pallas import tpu as pltpu
from jax.sharding import PartitionSpec as P

MESH = pl.DeviceIdType.MESH
F32 = jnp.float32
BF16 = jnp.bfloat16
I32 = jnp.int32

NODES = 3
ZS = 8
YS = 4
CHIPS = 8
ROWS = 16
PIECE = 32
T_WORDS = 136
G_WORDS = 72


def scale_of(code):
    value = code.astype(F32)
    return jnp.where(code > 0, value * (2.0**-8), value * (-(2.0**-30)))


def pack_into(ref, x):
    rows = x.shape[0]
    top = jnp.max(jnp.max(jnp.abs(x), axis=0, keepdims=True), axis=1, keepdims=True)
    coarse = jnp.ceil(top * 256.0).astype(I32)
    fine = -jnp.maximum(jnp.ceil(jnp.minimum(top, 1.0) * (2.0**30)), 1.0).astype(I32)
    code = jnp.where(top >= 1.0, coarse, fine)
    inverse = 32767.0 / scale_of(code)
    q = jnp.floor(x * inverse + 0.5).astype(I32)
    for half in range(2):
        upper = q[:, half * 128 : half * 128 + 128]
        lower = q[:, 256 + half * 128 : 384 + half * 128]
        ref[half * rows : half * rows + rows, :] = (upper << 16) | (lower & 0xFFFF)
    ref[2 * rows : 2 * rows + 8, :] = jnp.broadcast_to(code, (8, 128))


def unpack(ref, rows):
    step = scale_of(ref[2 * rows : 2 * rows + 8, :])[0:1, :] * (1.0 / 32767.0)
    parts = []
    words = [ref[half * rows : half * rows + rows, :] for half in range(2)]
    for word in words:
        parts.append((word >> 16).astype(F32) * step)
    for word in words:
        parts.append(((word << 16) >> 16).astype(F32) * step)
    return jnp.concatenate(parts, axis=1)


def kernel(
    blocks, factor_in, mask, cols_out, diag_out,
    raw, dense, factor, middle, gathered, row_factor, term, split, other, send_t, recv_t, cols,
    own_g, other_g, send_g, recv_g, tiles, recv_tiles, final, packed, diag,
    a_sem, l_sem, p_sem, q_sem, r_sem, m_sem, ring_send, ring_recv, core_send, core_recv,
    t_sem, c_sem, d_sem, g_sem, u_sem, f_sem, h_sem, k_sem, o_sem,
):
    r = lax.axis_index("prow")
    c = lax.axis_index("pcol")
    x_lo, z = r // ZS, r % ZS
    x_hi, y, core = c // (2 * YS), (c // 2) % YS, c % 2
    chip = c // 2
    mate = (r, chip * 2 + (1 - core))
    shift = y + YS * core
    origin = (z + ZS - shift) % ZS
    target = x_lo * ZS + origin

    def slot_at(where):
        gap = (where + ZS - c % ZS) % ZS
        return (gap % YS) * 2 + gap // YS

    def row_peer(d):
        return ((x_lo + d // ZS) % 2) * ZS + (z + d % ZS) % ZS

    def chip_peer(d):
        return ((x_hi + d // YS) % 2) * YS + (y + d % YS) % YS

    def remote(src, dst, send, recv, where):
        return pltpu.make_async_remote_copy(
            src_ref=src, dst_ref=dst, send_sem=send, recv_sem=recv, device_id=where, device_id_type=MESH
        )

    def landed(ref, sem):
        pltpu.make_async_copy(ref, ref, sem).wait()

    own_load = pltpu.make_async_copy(factor_in, factor, l_sem.at[0])
    own_load.start()
    loads = [
        pltpu.make_async_copy(blocks.at[s], raw.at[s], a_sem.at[s]) for s in range(NODES)
    ]
    for load in loads:
        load.start()

    barrier = pltpu.get_barrier_semaphore()

    def greet(where):
        pl.semaphore_signal(barrier, inc=1, device_id=where, device_id_type=MESH)

    same_lo = (r, target)
    other_lo = ((r + ZS) % ROWS, target)
    sources = [((c // ZS) * ZS + z, half * ZS + slot_at(z)) for half in range(2)]

    @pl.when(c != target)
    def _():
        greet(same_lo)

    greet(other_lo)
    for source in sources:
        mine = jnp.logical_and(source[0] == r, source[1] == c)

        @pl.when(jnp.logical_not(mine))
        def _():
            greet(source)

    greet(mate)

    def greet_row(d, carry):
        greet((row_peer(d), c))
        return carry

    lax.fori_loop(1, ROWS, greet_row, 0)

    def greet_chip(d, carry):
        greet((r, chip_peer(d) * 2 + core))
        return carry

    lax.fori_loop(1, CHIPS, greet_chip, 0)
    own_load.wait()

    @pl.when(c != target)
    def _():
        pl.semaphore_wait(barrier, 4 + 1 + (ROWS - 1) + (CHIPS - 1))

    @pl.when(c == target)
    def _():
        pl.semaphore_wait(barrier, 2 + 1 + (ROWS - 1) + (CHIPS - 1))

    def first_hop(s):
        where = (x_lo * ZS + (z + shift) % ZS, c)
        return remote(factor.at[s], middle.at[s], p_sem.at[s, 0], p_sem.at[s, 1], where)

    for s in range(NODES):

        @pl.when(shift != 0)
        def _():
            first_hop(s).start()

        @pl.when(shift == 0)
        def _():
            pltpu.make_async_copy(factor.at[s], middle.at[s], p_sem.at[s, 1]).start()

    def second_hop(s, way):
        where = same_lo if way == 0 else other_lo
        return remote(
            middle.at[s], gathered.at[s, :, c // ZS, c % ZS], q_sem.at[s, way], r_sem.at[s], where
        )

    def forward_piece(s):
        landed(middle.at[s], p_sem.at[s, 1])
        second_hop(s, 1).start()

        @pl.when(c != target)
        def _():
            second_hop(s, 0).start()

        @pl.when(c == target)
        def _():
            pltpu.make_async_copy(middle.at[s], gathered.at[s, :, c // ZS, c % ZS], r_sem.at[s]).start()

    def row_copy(s, d):
        return remote(
            factor.at[s], row_factor.at[s, :, chip, core], m_sem.at[s, 0], m_sem.at[s, 1],
            (r, chip_peer(d) * 2 + core),
        )

    def spread_rows(s):
        def body(d, carry):
            row_copy(s, d).start()
            return carry

        lax.fori_loop(1, CHIPS, body, 0)
        row_factor[s, :, chip, core] = factor[s]

    def rows_copy(s):
        ref = row_factor.at[s, :, :, core]
        return remote(ref, ref, m_sem.at[s, 2], m_sem.at[s, 3], mate)

    def share_rows(s):
        landed(row_factor.at[s, :, pl.ds(0, CHIPS - 1), core], m_sem.at[s, 1])
        rows_copy(s).start()

    right = (x_lo * ZS + (z + 1) % ZS, c)
    left = (x_lo * ZS + (z + ZS - 1) % ZS, c)

    def ring_copy(s, q, k, way):
        if way == 0:
            shard, where = slot_at((z + ZS - (k - 1)) % ZS), right
        else:
            shard, where = slot_at((z + (k - 1)) % ZS), left
        ref = gathered.at[s, q, :, shard]
        return remote(ref, ref, ring_send.at[s, q, way, k - 1], ring_recv.at[s, q, way, k - 1], where)

    def ring_landed(s, q, k, way):
        if way == 0:
            shard = slot_at((z + ZS - k) % ZS)
        else:
            shard = slot_at((z + k) % ZS)
        landed(gathered.at[s, q, :, shard], ring_recv.at[s, q, way, k - 1])

    def ring(s, k):
        if k == 1:
            landed(gathered.at[s, :, :, slot_at(z)], r_sem.at[s])
        for q in range(2):
            for way in range(2):
                if 1 < k < 5 or (k == 5 and way == q):
                    ring_landed(s, q, k - 1, way)
                if k < 4 or (k == 4 and way == q):
                    ring_copy(s, q, k, way).start()

    def separate(s, m):
        if m == 0:
            loads[s].wait()

        def body(i, carry):
            at = pl.multiple_of(i * 64, 64)
            for q in range(2):
                dense[s, m, q, pl.ds(at, 64), :] = raw[s, m, pl.ds(at, 64), q, :]
            return carry

        lax.fori_loop(0, 8, body, 0)

    def core_copy(s, m):
        return remote(
            term.at[s, m, :, 1 - core], other.at[s, m], core_send.at[s, m], core_recv.at[s, m], mate
        )

    def products(s):
        keep = [
            [-mask[s, m * ROWS + r, q * ROWS + c].astype(F32) for q in range(2)]
            for m in range(2)
        ]
        for m in range(2):
            def body(i, carry):
                at = pl.multiple_of(i * 256, 256)
                total = None
                for q in range(2):
                    right_side = gathered[s, q].reshape(512, 512)
                    part = keep[m][q] * jnp.dot(
                        dense[s, m, q, pl.ds(at, 256), :], right_side, preferred_element_type=F32
                    )
                    total = part if total is None else total + part
                term[s, m, pl.ds(i * 4, 4)] = total.reshape(4, 2, PIECE, 512)
                high = total.astype(BF16)
                split[m, 0, pl.ds(at, 256), :] = high
                split[m, 1, pl.ds(at, 256), :] = (total - high.astype(F32)).astype(BF16)
                return carry

            lax.fori_loop(0, 2, body, 0)
            core_copy(s, m).start()

    def t_copy(s, d):
        p = chip_peer(d)
        return remote(
            send_t.at[s, d - 1], recv_t.at[s, d - 1], t_sem.at[s, 0], t_sem.at[s, 1], (r, p * 2 + core)
        )

    def send_partials(s):
        for m in range(2):
            landed(other.at[s, m], core_recv.at[s, m])

        def body(d, carry):
            p = chip_peer(d)
            x = jnp.concatenate([term[s, m, p, core] + other[s, m, p] for m in range(2)], axis=0)
            pack_into(send_t.at[s, d - 1], x)
            t_copy(s, d).start()
            return carry

        lax.fori_loop(1, CHIPS, body, 0)
        for m in range(2):
            cols[s, m] = term[s, m, chip, core] + other[s, m, chip]

    def cols_copy(s):
        return pltpu.make_async_copy(cols.at[s], cols_out.at[s], c_sem.at[s])

    def sum_columns(s):
        landed(recv_t.at[s], t_sem.at[s, 1])

        def body(d, carry):
            cols[s] += unpack(recv_t.at[s, d], 64).reshape(2, PIECE, 512)
            return carry

        lax.fori_loop(0, CHIPS - 1, body, 0)
        cols_copy(s).start()

    def half_copy(s):
        return remote(own_g.at[s, 1 - core], other_g.at[s], d_sem.at[s, 0], d_sem.at[s, 1], mate)

    def diagonal_terms(s):
        landed(row_factor.at[s, :, :, 1 - core], m_sem.at[s, 3])
        for half in (1 - core, core):
            total = None
            for m in range(2):
                at = pl.multiple_of(half * 256, 256)
                left_side = row_factor[s, m, :, :, :, pl.ds(at, 256)].reshape(512, 256)
                for part in range(2):
                    dot = lax.dot_general(
                        left_side, split[m, part], (((0,), (0,)), ((), ())), preferred_element_type=F32
                    )
                    total = dot if total is None else total + dot
            own_g[s, half] = total
            if half is not core:
                half_copy(s).start()

    def g_copy(s, d):
        p = chip_peer(d)
        return remote(
            send_g.at[s, d - 1], recv_g.at[s, d - 1], g_sem.at[s, 0], g_sem.at[s, 1], (r, p * 2 + core)
        )

    def send_terms(s):
        landed(other_g.at[s], d_sem.at[s, 1])

        def body(d, carry):
            at = pl.multiple_of(chip_peer(d) * PIECE, PIECE)
            pack_into(send_g.at[s, d - 1], own_g[s, core, pl.ds(at, PIECE), :] + other_g[s, pl.ds(at, PIECE), :])
            g_copy(s, d).start()
            return carry

        lax.fori_loop(1, CHIPS, body, 0)

    def u_copy(s, d):
        return remote(
            tiles.at[s, row_peer(d)], recv_tiles.at[s, d - 1], u_sem.at[s, 0], u_sem.at[s, 1], (row_peer(d), c)
        )

    def send_tiles(s):
        landed(recv_g.at[s], g_sem.at[s, 1])
        own = pl.ds(pl.multiple_of(chip * PIECE, PIECE), PIECE)
        mine = own_g[s, core, own, :] + other_g[s, own, :]
        total = lax.fori_loop(0, CHIPS - 1, lambda d, x: x + unpack(recv_g.at[s, d], PIECE), mine)
        for i in range(4):
            for j in range(4):
                tiles[s, i * 4 + j] = total[i * 8 : i * 8 + 8, j * 128 : j * 128 + 128]

        def body(d, carry):
            u_copy(s, d).start()
            return carry

        lax.fori_loop(1, ROWS, body, 0)

    def f_copy(s, d):
        ref = final.at[s, r]
        return remote(ref, ref, f_sem.at[s, 0], f_sem.at[s, 1], (row_peer(d), c))

    def sum_tiles(s):
        landed(recv_tiles.at[s], u_sem.at[s, 1])
        final[s, r] = lax.fori_loop(0, ROWS - 1, lambda d, x: x + recv_tiles[s, d], tiles[s, r])

        def body(d, carry):
            f_copy(s, d).start()
            return carry

        lax.fori_loop(1, ROWS, body, 0)

    def h_copy(s, d):
        ref = packed.at[s, core, chip]
        return remote(ref, ref, h_sem.at[s, 0], h_sem.at[s, 1], (r, chip_peer(d) * 2 + core))

    def send_diagonal(s):
        landed(recv_tiles.at[s], f_sem.at[s, 1])
        rows = [jnp.concatenate([final[s, i * 4 + j] for j in range(4)], axis=1) for i in range(4)]
        pack_into(packed.at[s, core, chip], jnp.concatenate(rows, axis=0))

        def body(d, carry):
            h_copy(s, d).start()
            return carry

        lax.fori_loop(1, CHIPS, body, 0)

    def k_copy(s):
        ref = packed.at[s, core]
        return remote(ref, ref, k_sem.at[s, 0], k_sem.at[s, 1], mate)

    def share_diagonal(s):
        landed(recv_g.at[s], h_sem.at[s, 1])
        k_copy(s).start()

    def out_copy(s):
        return pltpu.make_async_copy(diag.at[s], diag_out.at[s], o_sem.at[s])

    def write_diagonal(s):
        landed(packed.at[s, 1 - core], k_sem.at[s, 1])

        def body(p, carry):
            for half in range(2):
                at = pl.multiple_of(half * 256 + p * PIECE, PIECE)
                diag[s, pl.ds(at, PIECE), :] = unpack(packed.at[s, half, p], PIECE)
            return carry

        lax.fori_loop(0, CHIPS, body, 0)
        out_copy(s).start()

    stage = {
        "D": separate, "P": forward_piece, "A": spread_rows, "F": share_rows, "R": ring,
        "1": products, "2": send_partials, "3": sum_columns, "4": diagonal_terms, "5": send_terms,
        "6": send_tiles, "7": sum_tiles, "8": send_diagonal, "9": share_diagonal, "W": write_diagonal,
    }
    order = (
        "D00", "P0", "A0", "D01", "P1", "A1", "R01", "P2", "A2", "R11", "D10", "R02",
        "D11", "R12", "F0", "R03", "R21", "D20", "R04", "R13", "R22", "D21", "F1", "R05",
        "10", "R14", "40", "R23", "R15", "50", "20", "R24", "F2", "11", "41", "R25",
        "51", "12", "42", "52", "21", "60", "22", "30", "61", "70", "31", "62",
        "71", "80", "72", "81", "90", "32", "82", "91", "W0", "92", "W1", "W2",
    )
    for word in order:
        stage[word[0]](*(int(n) for n in word[1:]))

    for s in range(NODES):

        @pl.when(shift != 0)
        def _():
            first_hop(s).wait_send()

        @pl.when(c != target)
        def _():
            second_hop(s, 0).wait_send()

        second_hop(s, 1).wait_send()
        landed(row_factor.at[s, :, pl.ds(0, CHIPS - 1), core], m_sem.at[s, 0])
        rows_copy(s).wait_send()
        for q in range(2):
            for k in range(1, 5):
                for way in range(2):
                    if k < 4 or way == q:
                        ring_copy(s, q, k, way).wait_send()
        for m in range(2):
            core_copy(s, m).wait_send()
        half_copy(s).wait_send()
        landed(send_t.at[s], t_sem.at[s, 0])
        landed(send_g.at[s], g_sem.at[s, 0])
        landed(recv_tiles.at[s], u_sem.at[s, 0])
        landed(recv_tiles.at[s], f_sem.at[s, 0])
        landed(recv_g.at[s], h_sem.at[s, 0])
        k_copy(s).wait_send()
        cols_copy(s).wait()
        out_copy(s).wait()


def shards(inverse_blocks, factor_cols, diag_inverse, block_mask):
    blocks = inverse_blocks.reshape(NODES, 2, 512, 2, 512)
    factor = factor_cols.reshape(NODES, 2, PIECE, 512)
    vmem = pltpu.VMEM
    dma = pltpu.SemaphoreType.DMA
    columns, term = pl.pallas_call(
        kernel,
        out_shape=(
            jax.ShapeDtypeStruct((NODES, 2, PIECE, 512), F32),
            jax.ShapeDtypeStruct((NODES, 512, 512), F32),
        ),
        in_specs=[
            pl.BlockSpec(memory_space=pl.ANY),
            pl.BlockSpec(memory_space=pl.ANY),
            pl.BlockSpec(memory_space=pltpu.SMEM),
        ],
        out_specs=(
            pl.BlockSpec(memory_space=pl.ANY),
            pl.BlockSpec(memory_space=pl.ANY),
        ),
        scratch_shapes=[
            vmem((NODES, 2, 512, 2, 512), BF16),
            vmem((NODES, 2, 2, 512, 512), BF16),
            vmem((NODES, 2, PIECE, 512), BF16),
            vmem((NODES, 2, PIECE, 512), BF16),
            vmem((NODES, 2, 2, ZS, PIECE, 512), BF16),
            vmem((NODES, 2, CHIPS, 2, PIECE, 512), BF16),
            vmem((NODES, 2, CHIPS, 2, PIECE, 512), F32),
            vmem((2, 2, 512, 512), BF16),
            vmem((NODES, 2, CHIPS, PIECE, 512), F32),
            vmem((NODES, CHIPS - 1, T_WORDS, 128), I32),
            vmem((NODES, CHIPS - 1, T_WORDS, 128), I32),
            vmem((NODES, 2, PIECE, 512), F32),
            vmem((NODES, 2, 256, 512), F32),
            vmem((NODES, 256, 512), F32),
            vmem((NODES, CHIPS - 1, G_WORDS, 128), I32),
            vmem((NODES, CHIPS - 1, G_WORDS, 128), I32),
            vmem((NODES, ROWS, 8, 128), F32),
            vmem((NODES, ROWS - 1, 8, 128), F32),
            vmem((NODES, ROWS, 8, 128), F32),
            vmem((NODES, 2, CHIPS, G_WORDS, 128), I32),
            vmem((NODES, 512, 512), F32),
            dma((NODES,)),
            dma((1,)),
            dma((NODES, 2)),
            dma((NODES, 2)),
            dma((NODES,)),
            dma((NODES, 4)),
            dma((NODES, 2, 2, 4)),
            dma((NODES, 2, 2, 4)),
            dma((NODES, 2)),
            dma((NODES, 2)),
            dma((NODES, 2)),
            dma((NODES,)),
            dma((NODES, 2)),
            dma((NODES, 2)),
            dma((NODES, 2)),
            dma((NODES, 2)),
            dma((NODES, 2)),
            dma((NODES, 2)),
            dma((NODES,)),
        ],
        compiler_params=pltpu.CompilerParams(
            collective_id=0, has_side_effects=True, vmem_limit_bytes=48 * 2**20
        ),
        cost_estimate=pl.CostEstimate(
            flops=NODES * 4 * 2 * 512**3, bytes_accessed=16 * 2**20, transcendentals=0
        ),
    )(blocks, factor, block_mask)
    inverse_cols = columns.reshape(NODES, 2, 1, PIECE, 512)
    return (inverse_cols, diag_inverse - term)


def solution(mesh):
    placed = (
        P(None, None, "prow", None, None, "pcol", None),
        P(None, None, "prow", "pcol", None),
        P(),
        P(),
    )
    return jax.shard_map(
        shards,
        mesh=mesh,
        in_specs=placed,
        out_specs=(P(None, None, "prow", "pcol", None), P()),
        check_vma=False,
    )
```

time: 608 us -> 122 us (0.20)
  waiting for transfers between devices: 558 us -> 0 us
  Pallas kernels: 0 us -> 116 us
  matrix products: 13.9 us -> 0 us
  between operations: 13.8 us -> 0.66 us
  other arithmetic: 14.4 us -> 2.41 us
    psum x2 -> x0, waiting for transfers between devices: 392 us -> none  [the longest x1 263 us: shards(): lax.psum(jnp.einsum('smaw,smav->swv', owned_rows, columns, precision=high...]
    pallas_call x0 -> x1, Pallas kernels: none -> 116 us  [shards(): pl.pallas_call(kernel, out_shape=(jax.ShapeDtypeStruct((NODES, 2, PIECE,...]
    reduce_scatter x1 -> x0, waiting for transfers between devices: 103 us -> none  [shards(): columns = lax.psum_scatter(term, 'pcol', scatter_dimension=2, tiled=True)]
    all_gather x1 -> x0, waiting for transfers between devices: 62.9 us -> none  [shards(): row_group = lax.all_gather(factor_cols, 'pcol', axis=3, tiled=True)]
    dot_general x2 -> x0, matrix products: 13.9 us -> none  [the longest x1 9.77 us: shards(): jnp.einsum('smaqb,sqbw->smaw', local, col_group, preferred_element_type=j...]
    mul x2 -> x0, other arithmetic: 8.24 us -> none  [shards(): local = local * owned_mask[:, :, None, :, None].astype(jnp.bfloat16)]
  transfers between devices with their start and end apart: 4 -> 0, of which waited for: 4 -> 0; matrix products, arithmetic and copies ran while one was open for 2% -> 0% of each run, Pallas kernels for 0% -> 0%
where the time goes in v1:
time: 122 us
  Pallas kernels  116 us (95%)
  local copies, waits for them, and re-layouts  2.47 us (2%)
  other arithmetic  2.41 us (2%)
    pallas_call x1, Pallas kernels, shards(): pl.pallas_call(kernel, out_shape=(jax.ShapeDtypeStruct((NODES, 2, PIECE,...  116 us
    unnamed x7, local copies, waits for them, and re-layouts  2.47 us

profile of v1, /device:TPU:1, one launch (start us, length us, event | category | flops | bytes accessed | tf_op | source)
XLA Modules:
  0.0 121.7 jit_solution(15276229745139426042)
XLA Ops:
  0.6 0.0 copy-start
  0.6 0.9 copy-done
  1.6 0.0 copy-start.1
  1.6 0.8 copy-done.1
  2.4 0.0 copy-start.2
  2.4 116.2 %shard_map.59 = (f32[3,2,32,512]{3,2,1,0:T(8,128)S(1)}, f32[3,512,512]{2,1,0:T(8,128)S(1)}) custom-call(bf16[3,2,512,2,512]{4,3,2,1,0:T(2,128)(2,1)} %bitcast.7, bf16[3,2,32,512]{3,2,1,0:T(8,128)(2,1)S(1)} %bitcast.6, s32[3,32,32]{2,1,0:T(8,128)S(1)} %copy-done.1), custom_call_target="tpu_custom_call" | custom-call | flops 3221225472 | bytes 16777216 | tf_op jit(solution)/shard_map/pallas_call | solution.py:457
  118.5 0.0 copy-done.2
  118.6 2.4 %sub.3 = f32[3,512,512]{2,1,0:T(8,128)} subtract(f32[3,512,512]{2,1,0:T(8,128)S(1)} %copy-done.2, f32[3,512,512]{2,1,0:T(8,128)S(1)} %get-tuple-element.5) | non-fusion elementwise | flops 786432 | bytes 9437184 | tf_op jit(solution)/shard_map/sub | solution.py:522
  121.0 0.7 copy.8
Async XLA Ops:
  0.6 0.9 copy-start
  1.6 0.8 copy-start.1
  2.4 116.2 %copy-start.2 = (f32[3,512,512]{2,1,0:T(8,128)S(1)}, f32[3,512,512]{2,1,0:T(8,128)}, u32[]{:S(2)}) copy-start(f32[3,512,512]{2,1,0:T(8,128)} %param.6) | copy-start | bytes 9437188

commit v2 on v1

v2 whole, which is shorter than its diff:
```python
import jax
import jax.numpy as jnp
from jax import lax
from jax.experimental import pallas as pl
from jax.experimental.pallas import tpu as pltpu
from jax.sharding import PartitionSpec as P

MESH = pl.DeviceIdType.MESH
F32 = jnp.float32
BF16 = jnp.bfloat16
I32 = jnp.int32

NODES = 3
ZS = 8
YS = 4
CHIPS = 8
ROWS = 16
PLANE = 16
FIRST = 0
PIECE = 32
T_WORDS = 136
G_WORDS = 40


def scale_of(code):
    value = code.astype(F32)
    return jnp.where(code > 0, value * (2.0**-8), value * (-(2.0**-30)))


def code_of(top):
    coarse = jnp.ceil(top * 256.0).astype(I32)
    fine = -jnp.maximum(jnp.ceil(jnp.minimum(top, 1.0) * (2.0**30)), 1.0).astype(I32)
    return jnp.where(top >= 1.0, coarse, fine)


def largest(x):
    return jnp.max(jnp.max(jnp.abs(x), axis=0, keepdims=True), axis=1, keepdims=True)


def pack_into(ref, x, code):
    rows = x.shape[0]
    inverse = 32767.0 / scale_of(code)
    q = jnp.floor(x * inverse + 0.5).astype(I32)
    for half in range(2):
        upper = q[:, half * 128 : half * 128 + 128]
        lower = q[:, 256 + half * 128 : 384 + half * 128]
        ref[half * rows : half * rows + rows, :] = (upper << 16) | (lower & 0xFFFF)
    ref[2 * rows : 2 * rows + 8, :] = jnp.broadcast_to(code, (8, 128))


def unpack(ref, rows):
    step = scale_of(ref[2 * rows : 2 * rows + 8, :])[0:1, :] * (1.0 / 32767.0)
    parts = []
    words = [ref[half * rows : half * rows + rows, :] for half in range(2)]
    for word in words:
        parts.append((word >> 16).astype(F32) * step)
    for word in words:
        parts.append(((word << 16) >> 16).astype(F32) * step)
    return jnp.concatenate(parts, axis=1)


def kernel(
    blocks, factor_in, mask_in, cols_out, diag_out,
    raw, dense, factor, middle, column, gathered, row_factor, term, split, other, send_t, recv_t, cols,
    own_g, other_g, send_g, recv_g, levels, packed, diag, mask,
    a_sem, l_sem, p_sem, q_sem, r_sem, z_sem, y_sem, m_sem, ring_send, ring_recv, core_send, core_recv,
    t_sem, c_sem, d_sem, g_sem, u_sem, h_sem, k_sem, o_sem,
):
    r = lax.axis_index("prow")
    c = lax.axis_index("pcol")
    x_lo, z = r // ZS, r % ZS
    x_hi, y, core = c // (2 * YS), (c // 2) % YS, c % 2
    chip = c // 2
    mate = (r, chip * 2 + (1 - core))
    shift = y + YS * core
    origin = (z + ZS - shift) % ZS
    target = x_lo * ZS + origin

    def slot_at(where):
        gap = (where + ZS - c % ZS) % ZS
        return (gap % YS) * 2 + gap // YS

    def z_peer(d):
        j = d - 1
        step = 4 + j // 2 - (j % 2) * (2 * (j // 2) + 1)
        return x_lo * ZS + (z + step + ZS) % ZS

    place_here = (x_lo * 2 + x_hi) * YS + y

    def plane_peer(d):
        i, j = (d - 1) % 4, (d - 1) // 4
        step = 2 + j // 2 - (j % 2) * (2 * (j // 2) + 1)
        return (x_lo + (i + 1) // 2) % 2, (x_hi + 1 - i // 2) % 2, (y + step + YS) % YS

    def plane_device(d):
        lo, hi, at_y = plane_peer(d)
        return (lo * ZS + z, hi * (2 * YS) + at_y * 2 + core)

    def plane_place(d):
        lo, hi, at_y = plane_peer(d)
        return (lo * 2 + hi) * YS + at_y

    def chip_peer(d):
        j = (d - 1) // 2
        step = 2 + j // 2 - (j % 2) * (2 * (j // 2) + 1)
        return ((x_hi + d % 2) % 2) * YS + (y + step + YS) % YS

    def remote(src, dst, send, recv, where):
        return pltpu.make_async_remote_copy(
            src_ref=src, dst_ref=dst, send_sem=send, recv_sem=recv, device_id=where, device_id_type=MESH
        )

    def landed(ref, sem):
        pltpu.make_async_copy(ref, ref, sem).wait()

    own_load = pltpu.make_async_copy(factor_in, factor, l_sem.at[0])
    own_load.start()
    mask_load = pltpu.make_async_copy(mask_in, mask, l_sem.at[1])
    mask_load.start()
    loads = [
        pltpu.make_async_copy(blocks.at[s], raw.at[s], a_sem.at[s]) for s in range(NODES)
    ]
    for load in loads:
        load.start()

    barrier = pltpu.get_barrier_semaphore()

    def greet(where):
        pl.semaphore_signal(barrier, inc=1, device_id=where, device_id_type=MESH)

    same_lo = (r, target)
    other_lo = ((r + ZS) % ROWS, target)
    has_self = c == target if FIRST == 0 else c // ZS == x_lo
    rounds = 1 if FIRST == 0 else ZS

    def greet_plane(i, carry):
        for lo in range(2):
            if FIRST == 0:
                there = (lo * ZS + z, target)
                back = ((c // ZS) * ZS + z, lo * ZS + slot_at(z))
            else:
                there = (lo * ZS + z, x_lo * ZS + i)
                back = ((c // ZS) * ZS + z, lo * ZS + i)

            @pl.when(jnp.logical_not(jnp.logical_and(there[0] == r, there[1] == c)))
            def _():
                greet(there)

            @pl.when(jnp.logical_not(jnp.logical_and(back[0] == r, back[1] == c)))
            def _():
                greet(back)

        return carry

    lax.fori_loop(0, rounds, greet_plane, 0)
    greet(mate)

    def greet_z(d, carry):
        greet((z_peer(d), c))
        return carry

    lax.fori_loop(1, ZS, greet_z, 0)

    def greet_xy(d, carry):
        greet(plane_device(d))
        return carry

    lax.fori_loop(1, PLANE, greet_xy, 0)
    own_load.wait()

    partners = 4 * rounds + 1 + (ZS - 1) + (PLANE - 1)

    @pl.when(jnp.logical_not(has_self))
    def _():
        pl.semaphore_wait(barrier, partners)

    @pl.when(has_self)
    def _():
        pl.semaphore_wait(barrier, partners - 2)

    def first_hop(s):
        where = (x_lo * ZS + (z + shift) % ZS, c)
        return remote(factor.at[s], middle.at[s], p_sem.at[s, 0], p_sem.at[s, 1], where)

    right = (x_lo * ZS + (z + 1) % ZS, c)
    left = (x_lo * ZS + (z + ZS - 1) % ZS, c)

    def column_copy(k, way):
        if way == 0:
            begun, where = (z + ZS - (k - 1)) % ZS, right
        else:
            begun, where = (z + (k - 1)) % ZS, left
        ref = column.at[begun] if k < 4 else column.at[begun, way]
        src = ref if k > 1 else factor.at[0]
        return remote(src, ref, z_sem.at[0, way, k - 1], z_sem.at[1, way, k - 1], where)

    def column_landed(k, way):
        begun = (z + ZS - k) % ZS if way == 0 else (z + k) % ZS
        landed(column.at[begun] if k < 4 else column.at[begun, way], z_sem.at[1, way, k - 1])

    def place_copy(i, lo):
        begun = (z + i) % ZS
        src = factor.at[0] if i == 0 else column.at[begun]
        where = (((x_lo + lo) % 2) * ZS + z, x_lo * ZS + begun)
        return remote(src, gathered.at[0, :, c // ZS, c % ZS], y_sem.at[i, lo], r_sem.at[0], where)

    def place(i):
        begun = (z + i) % ZS
        place_copy(i, 1).start()

        @pl.when(c != x_lo * ZS + begun)
        def _():
            place_copy(i, 0).start()

        @pl.when(c == x_lo * ZS + begun)
        def _():
            src = factor.at[0] if i == 0 else column.at[begun]
            pltpu.make_async_copy(src, gathered.at[0, :, c // ZS, c % ZS], r_sem.at[0]).start()

    def around(k):
        for way in range(2):
            if k > 1:
                column_landed(k - 1, way)
            if k < 5:
                column_copy(k, way).start()
        if k == 1:
            place(0)
        elif k < 5:
            place(ZS - (k - 1))
            place(k - 1)
        else:
            place(4)

    if FIRST:
        around(1)
    for s in range(FIRST, NODES):

        @pl.when(shift != 0)
        def _():
            first_hop(s).start()

        @pl.when(shift == 0)
        def _():
            pltpu.make_async_copy(factor.at[s], middle.at[s], p_sem.at[s, 1]).start()

    def second_hop(s, way):
        where = same_lo if way == 0 else other_lo
        return remote(
            middle.at[s], gathered.at[s, :, c // ZS, c % ZS], q_sem.at[s, way], r_sem.at[s], where
        )

    def forward_piece(s):
        landed(middle.at[s], p_sem.at[s, 1])
        second_hop(s, 1).start()

        @pl.when(c != target)
        def _():
            second_hop(s, 0).start()

        @pl.when(c == target)
        def _():
            pltpu.make_async_copy(middle.at[s], gathered.at[s, :, c // ZS, c % ZS], r_sem.at[s]).start()

    across = (r, ((x_hi + 1) % 2) * (2 * YS) + y * 2 + core)

    def across_copy(s):
        return remote(
            factor.at[s], row_factor.at[s, x_hi, y, core], m_sem.at[s, 0], m_sem.at[s, 1], across
        )

    def cross_rows(s):
        across_copy(s).start()
        row_factor[s, x_hi, y, core] = factor[s]

    def row_copy(s, d):
        ref = row_factor.at[s, :, y, core]
        where = (r, x_hi * (2 * YS) + ((y + d) % YS) * 2 + core)
        return remote(ref, ref, m_sem.at[s, 2], m_sem.at[s, 3], where)

    def spread_rows(s):
        landed(row_factor.at[s, 1 - x_hi, y, core], m_sem.at[s, 1])
        for d in (2, 1, 3):
            row_copy(s, d).start()

    def rows_copy(s):
        ref = row_factor.at[s, :, :, core]
        return remote(ref, ref, m_sem.at[s, 4], m_sem.at[s, 5], mate)

    def share_rows(s):
        landed(row_factor.at[s, :, pl.ds(0, YS - 1), core], m_sem.at[s, 3])
        rows_copy(s).start()

    def ring_copy(s, q, k, way):
        if way == 0:
            shard, where = slot_at((z + ZS - (k - 1)) % ZS), right
        else:
            shard, where = slot_at((z + (k - 1)) % ZS), left
        ref = gathered.at[s, q, :, shard]
        return remote(ref, ref, ring_send.at[s, q, way, k - 1], ring_recv.at[s, q, way, k - 1], where)

    def ring_landed(s, q, k, way):
        if way == 0:
            shard = slot_at((z + ZS - k) % ZS)
        else:
            shard = slot_at((z + k) % ZS)
        landed(gathered.at[s, q, :, shard], ring_recv.at[s, q, way, k - 1])

    def ring(s, k):
        if k == 1:
            landed(gathered.at[s, :, :, slot_at(z)], r_sem.at[s])
        for q in range(2):
            for way in range(2):
                if 1 < k < 5 or (k == 5 and way == q):
                    ring_landed(s, q, k - 1, way)
                if k < 4 or (k == 4 and way == q):
                    ring_copy(s, q, k, way).start()

    def separate(s, m):
        if m == 0:
            loads[s].wait()

        def body(i, carry):
            at = pl.multiple_of(i * 64, 64)
            for q in range(2):
                dense[s, m, q, pl.ds(at, 64), :] = raw[s, m, pl.ds(at, 64), q, :]
            return carry

        lax.fori_loop(0, 8, body, 0)

    def core_copy(s, m):
        return remote(
            term.at[s, m, :, 1 - core], other.at[s, m], core_send.at[s, m], core_recv.at[s, m], mate
        )

    def products(s):
        if s < FIRST:
            landed(gathered.at[0], r_sem.at[0])
        if s == 0:
            mask_load.wait()
        keep = [
            [-mask[s, m * ROWS + r, q * ROWS + c].astype(F32) for q in range(2)]
            for m in range(2)
        ]
        for m in range(2):
            def body(i, carry):
                at = pl.multiple_of(i * 256, 256)
                total = None
                for q in range(2):
                    right_side = gathered[s, q].reshape(512, 512)
                    part = keep[m][q] * jnp.dot(
                        dense[s, m, q, pl.ds(at, 256), :], right_side, preferred_element_type=F32
                    )
                    total = part if total is None else total + part
                term[s, m, pl.ds(i * 4, 4)] = total.reshape(4, 2, PIECE, 512)
                high = total.astype(BF16)
                split[m, 0, pl.ds(at, 256), :] = high
                split[m, 1, pl.ds(at, 256), :] = (total - high.astype(F32)).astype(BF16)
                return carry

            lax.fori_loop(0, 2, body, 0)
            core_copy(s, m).start()

    def t_copy(s, d):
        p = chip_peer(d)
        return remote(
            send_t.at[s, d - 1], recv_t.at[s, d - 1], t_sem.at[s, 0], t_sem.at[s, 1], (r, p * 2 + core)
        )

    def send_partials(s):
        for m in range(2):
            landed(other.at[s, m], core_recv.at[s, m])

        def join(p, top):
            for m in range(2):
                x = term[s, m, p, core] + other[s, m, p]
                term[s, m, p, core] = x
                top = jnp.maximum(top, jnp.abs(x))
            return top

        code = code_of(largest(lax.fori_loop(0, CHIPS, join, jnp.zeros((PIECE, 512), F32))))

        def body(d, carry):
            p = chip_peer(d)
            x = jnp.concatenate([term[s, m, p, core] for m in range(2)], axis=0)
            pack_into(send_t.at[s, d - 1], x, code)
            t_copy(s, d).start()
            return carry

        lax.fori_loop(1, CHIPS, body, 0)
        for m in range(2):
            cols[s, m] = term[s, m, chip, core]

    def cols_copy(s):
        return pltpu.make_async_copy(cols.at[s], cols_out.at[s], c_sem.at[s])

    def sum_columns(s):
        landed(recv_t.at[s], t_sem.at[s, 1])

        def body(d, carry):
            cols[s] += unpack(recv_t.at[s, d], 64).reshape(2, PIECE, 512)
            return carry

        lax.fori_loop(0, CHIPS - 1, body, 0)
        cols_copy(s).start()

    def half_copy(s):
        return remote(own_g.at[s, 1 - core], other_g.at[s], d_sem.at[s, 0], d_sem.at[s, 1], mate)

    def diagonal_terms(s):
        landed(row_factor.at[s, :, :, 1 - core], m_sem.at[s, 5])
        for half in (1 - core, core):
            total = None
            for m in range(2):
                at = pl.multiple_of(half * 256, 256)
                left_side = row_factor[s, :, :, :, m, :, pl.ds(at, 256)].reshape(512, 256)
                for part in range(2):
                    dot = lax.dot_general(
                        left_side, split[m, part], (((0,), (0,)), ((), ())), preferred_element_type=F32
                    )
                    total = dot if total is None else total + dot
            own_g[s, half] = total
            if half is not core:
                half_copy(s).start()

    def g_copy(s, d):
        return remote(
            send_g.at[s, d - 1], recv_g.at[s, d - 1], g_sem.at[s, 0], g_sem.at[s, 1], plane_device(d)
        )

    def send_terms(s):
        landed(other_g.at[s], d_sem.at[s, 1])
        whole = own_g[s, core] + other_g[s]
        own_g[s, core] = whole
        code = code_of(largest(whole))

        def body(d, carry):
            at = pl.multiple_of(plane_place(d) * 16, 16)
            pack_into(send_g.at[s, d - 1], own_g[s, core, pl.ds(at, 16), :], code)
            g_copy(s, d).start()
            return carry

        lax.fori_loop(1, PLANE, body, 0)

    def u_copy(s, d):
        ref = levels.at[s, z]
        return remote(ref, ref, u_sem.at[s, 0], u_sem.at[s, 1], (z_peer(d), c))

    def send_levels(s):
        landed(recv_g.at[s], g_sem.at[s, 1])
        mine = own_g[s, core, pl.ds(pl.multiple_of(place_here * 16, 16), 16), :]
        total = lax.fori_loop(0, PLANE - 1, lambda d, x: x + unpack(recv_g.at[s, d], 16), mine)
        pack_into(levels.at[s, z], total, code_of(largest(total)))

        def body(d, carry):
            u_copy(s, d).start()
            return carry

        lax.fori_loop(1, ZS, body, 0)

    def h_copy(s, d):
        ref = packed.at[s, core, place_here]
        return remote(ref, ref, h_sem.at[s, 0], h_sem.at[s, 1], plane_device(d))

    def send_diagonal(s):
        landed(levels.at[s, pl.ds(0, ZS - 1)], u_sem.at[s, 1])
        zero = jnp.zeros((16, 512), F32)
        total = lax.fori_loop(0, ZS, lambda i, x: x + unpack(levels.at[s, i], 16), zero)
        pack_into(packed.at[s, core, place_here], total, code_of(largest(total)))

        def body(d, carry):
            h_copy(s, d).start()
            return carry

        lax.fori_loop(1, PLANE, body, 0)

    def k_copy(s):
        ref = packed.at[s, core]
        return remote(ref, ref, k_sem.at[s, 0], k_sem.at[s, 1], mate)

    def share_diagonal(s):
        landed(recv_g.at[s], h_sem.at[s, 1])
        k_copy(s).start()

    def out_copy(s):
        return pltpu.make_async_copy(diag.at[s], diag_out.at[s], o_sem.at[s])

    def write_diagonal(s):
        landed(packed.at[s, 1 - core], k_sem.at[s, 1])

        def body(p, carry):
            for half in range(2):
                at = pl.multiple_of(half * 256 + p * 16, 16)
                diag[s, pl.ds(at, 16), :] = unpack(packed.at[s, half, p], 16)
            return carry

        lax.fori_loop(0, PLANE, body, 0)
        out_copy(s).start()

    stage = {
        "D": separate, "Z": around, "P": forward_piece, "B": cross_rows, "A": spread_rows, "F": share_rows, "R": ring,
        "1": products, "2": send_partials, "3": sum_columns, "4": diagonal_terms, "5": send_terms,
        "6": send_levels, "7": send_diagonal, "8": share_diagonal, "9": write_diagonal,
    }
    order = (
        "B0", "B1", "B2", "D00", "D01", "P0", "A0", "D10", "P1", "D11", "R01", "A1",
        "P2", "D20", "R02", "R11", "D21", "R03", "R12", "A2", "F0", "R04", "R13", "F1",
        "R05", "R14", "10", "R21", "40", "F2", "R15", "R22", "20", "50", "11", "R23",
        "R24", "21", "41", "51", "60", "R25", "12", "42", "52", "70", "61", "30",
        "62", "22", "80", "71", "72", "31", "81", "90", "82", "91", "32", "92",
    )
    for word in order:
        stage[word[0]](*(int(n) for n in word[1:]))

    if FIRST:
        for k in range(1, 5):
            for way in range(2):
                column_copy(k, way).wait_send()
        for i in range(ZS):
            place_copy(i, 1).wait_send()

            @pl.when(c != x_lo * ZS + (z + i) % ZS)
            def _():
                place_copy(i, 0).wait_send()

    for s in range(NODES):
        if s >= FIRST:

            @pl.when(shift != 0)
            def _():
                first_hop(s).wait_send()

            @pl.when(c != target)
            def _():
                second_hop(s, 0).wait_send()

            second_hop(s, 1).wait_send()
            for q in range(2):
                for k in range(1, 5):
                    for way in range(2):
                        if k < 4 or way == q:
                            ring_copy(s, q, k, way).wait_send()
        across_copy(s).wait_send()
        landed(row_factor.at[s, :, pl.ds(0, YS - 1), core], m_sem.at[s, 2])
        rows_copy(s).wait_send()
        for m in range(2):
            core_copy(s, m).wait_send()
        half_copy(s).wait_send()
        landed(send_t.at[s], t_sem.at[s, 0])
        landed(send_g.at[s], g_sem.at[s, 0])
        landed(levels.at[s, pl.ds(0, ZS - 1)], u_sem.at[s, 0])
        landed(recv_g.at[s], h_sem.at[s, 0])
        k_copy(s).wait_send()
        cols_copy(s).wait()
        out_copy(s).wait()


def shards(inverse_blocks, factor_cols, diag_inverse, block_mask):
    blocks = inverse_blocks.reshape(NODES, 2, 512, 2, 512)
    factor = factor_cols.reshape(NODES, 2, PIECE, 512)
    vmem = pltpu.VMEM
    dma = pltpu.SemaphoreType.DMA
    columns, term = pl.pallas_call(
        kernel,
        out_shape=(
            jax.ShapeDtypeStruct((NODES, 2, PIECE, 512), F32),
            jax.ShapeDtypeStruct((NODES, 512, 512), F32),
        ),
        in_specs=[
            pl.BlockSpec(memory_space=pltpu.HBM),
            pl.BlockSpec(memory_space=pltpu.HBM),
            pl.BlockSpec(memory_space=pltpu.HBM),
        ],
        out_specs=(
            pl.BlockSpec(memory_space=pl.ANY),
            pl.BlockSpec(memory_space=pl.ANY),
        ),
        scratch_shapes=[
            vmem((NODES, 2, 512, 2, 512), BF16),
            vmem((NODES, 2, 2, 512, 512), BF16),
            vmem((NODES, 2, PIECE, 512), BF16),
            vmem((NODES, 2, PIECE, 512), BF16),
            vmem((ZS, 2, PIECE, 512), BF16),
            vmem((NODES, 2, 2, ZS, PIECE, 512), BF16),
            vmem((NODES, 2, YS, 2, 2, PIECE, 512), BF16),
            vmem((NODES, 2, CHIPS, 2, PIECE, 512), F32),
            vmem((2, 2, 512, 512), BF16),
            vmem((NODES, 2, CHIPS, PIECE, 512), F32),
            vmem((NODES, CHIPS - 1, T_WORDS, 128), I32),
            vmem((NODES, CHIPS - 1, T_WORDS, 128), I32),
            vmem((NODES, 2, PIECE, 512), F32),
            vmem((NODES, 2, 256, 512), F32),
            vmem((NODES, 256, 512), F32),
            vmem((NODES, PLANE - 1, G_WORDS, 128), I32),
            vmem((NODES, PLANE - 1, G_WORDS, 128), I32),
            vmem((NODES, ZS, G_WORDS, 128), I32),
            vmem((NODES, 2, PLANE, G_WORDS, 128), I32),
            vmem((NODES, 512, 512), F32),
            pltpu.SMEM((NODES, 32, 32), I32),
            dma((NODES,)),
            dma((2,)),
            dma((NODES, 2)),
            dma((NODES, 2)),
            dma((NODES,)),
            dma((2, 2, 4)),
            dma((ZS, 2)),
            dma((NODES, 6)),
            dma((NODES, 2, 2, 4)),
            dma((NODES, 2, 2, 4)),
            dma((NODES, 2)),
            dma((NODES, 2)),
            dma((NODES, 2)),
            dma((NODES,)),
            dma((NODES, 2)),
            dma((NODES, 2)),
            dma((NODES, 2)),
            dma((NODES, 2)),
            dma((NODES, 2)),
            dma((NODES,)),
        ],
        compiler_params=pltpu.CompilerParams(
            collective_id=0, has_side_effects=True, vmem_limit_bytes=48 * 2**20
        ),
        cost_estimate=pl.CostEstimate(
            flops=NODES * 4 * 2 * 512**3, bytes_accessed=16 * 2**20, transcendentals=0
        ),
    )(blocks, factor, block_mask)
    inverse_cols = columns.reshape(NODES, 2, 1, PIECE, 512)
    return (inverse_cols, diag_inverse - term)


def solution(mesh):
    placed = (
        P(None, None, "prow", None, None, "pcol", None),
        P(None, None, "prow", "pcol", None),
        P(),
        P(),
    )
    return jax.shard_map(
        shards,
        mesh=mesh,
        in_specs=placed,
        out_specs=(P(None, None, "prow", "pcol", None), P()),
        check_vma=False,
    )
```

time: 122 us -> 105 us (0.86)
  Pallas kernels: 116 us -> 99.7 us
    pallas_call x1, Pallas kernels: 116 us -> 99.7 us  [shards(): pl.pallas_call(kernel, out_shape=(jax.ShapeDtypeStruct((NODES, 2, PIECE,...]
where the time goes in v2:
time: 105 us
  Pallas kernels  99.7 us (95%)
  local copies, waits for them, and re-layouts  2.47 us (2%)
  other arithmetic  2.41 us (2%)
    pallas_call x1, Pallas kernels, shards(): pl.pallas_call(kernel, out_shape=(jax.ShapeDtypeStruct((NODES, 2, PIECE,...  99.7 us
    unnamed x7, local copies, waits for them, and re-layouts  2.47 us
    sub x1, other arithmetic, shards(): return (inverse_cols, diag_inverse - term)  2.41 us

profile of v2, /device:TPU:1, one launch (start us, length us, event | category | flops | bytes accessed | tf_op | source)
XLA Modules:
  0.0 105.2 jit_solution(12088753795013626364)
XLA Ops:
  0.6 0.0 copy-start
  0.6 0.9 copy-done
  1.6 0.0 copy-start.1
  1.6 0.8 copy-done.1
  2.4 0.0 copy-start.2
  2.4 99.7 %shard_map.59 = (f32[3,2,32,512]{3,2,1,0:T(8,128)S(1)}, f32[3,512,512]{2,1,0:T(8,128)S(1)}) custom-call(bf16[3,2,512,2,512]{4,3,2,1,0:T(2,128)(2,1)} %bitcast.7, bf16[3,2,32,512]{3,2,1,0:T(8,128)(2,1)S(1)} %bitcast.6, s32[3,32,32]{2,1,0:T(8,128)S(1)} %copy-done.1), custom_call_target="tpu_custom_call" | custom-call | flops 3221225472 | bytes 16777216 | tf_op jit(solution)/shard_map/pallas_call | solution.py:562
  102.1 0.0 copy-done.2
  102.1 2.4 %sub.3 = f32[3,512,512]{2,1,0:T(8,128)} subtract(f32[3,512,512]{2,1,0:T(8,128)S(1)} %copy-done.2, f32[3,512,512]{2,1,0:T(8,128)S(1)} %get-tuple-element.5) | non-fusion elementwise | flops 786432 | bytes 9437184 | tf_op jit(solution)/shard_map/sub | solution.py:628
  104.5 0.7 copy.8
Async XLA Ops:
  0.6 0.9 copy-start
  1.6 0.8 copy-start.1
  2.4 99.7 %copy-start.2 = (f32[3,512,512]{2,1,0:T(8,128)S(1)}, f32[3,512,512]{2,1,0:T(8,128)}, u32[]{:S(2)}) copy-start(f32[3,512,512]{2,1,0:T(8,128)} %param.6) | copy-start | bytes 9437188

commit v3 on v2

--- a/solution.py
+++ b/solution.py
@@ -17,6 +17,7 @@
 ROWS = 16
 PLANE = 16
 FIRST = 0
+SHARED = (1,)
 PIECE = 32
 T_WORDS = 136
 G_WORDS = 40
@@ -63,7 +64,7 @@
     blocks, factor_in, mask_in, cols_out, diag_out,
     raw, dense, factor, middle, column, gathered, row_factor, term, split, other, send_t, recv_t, cols,
     own_g, other_g, send_g, recv_g, levels, packed, diag, mask,
-    a_sem, l_sem, p_sem, q_sem, r_sem, z_sem, y_sem, m_sem, ring_send, ring_recv, core_send, core_recv,
+    a_sem, l_sem, p_sem, q_sem, r_sem, x_sem, z_sem, y_sem, m_sem, ring_send, ring_recv, core_send, core_recv,
     t_sem, c_sem, d_sem, g_sem, u_sem, h_sem, k_sem, o_sem,
 ):
     r = lax.axis_index("prow")
@@ -245,19 +246,25 @@
 
     def second_hop(s, way):
         where = same_lo if way == 0 else other_lo
+        if s in SHARED:
+            where = (x_hi * ZS + z, target)
         return remote(
             middle.at[s], gathered.at[s, :, c // ZS, c % ZS], q_sem.at[s, way], r_sem.at[s], where
         )
 
     def forward_piece(s):
         landed(middle.at[s], p_sem.at[s, 1])
-        second_hop(s, 1).start()
-
-        @pl.when(c != target)
+        stays = c == target
+        if s in SHARED:
+            stays = jnp.logical_and(stays, x_hi == x_lo)
+        else:
+            second_hop(s, 1).start()
+
+        @pl.when(jnp.logical_not(stays))
         def _():
             second_hop(s, 0).start()
 
-        @pl.when(c == target)
+        @pl.when(stays)
         def _():
             pltpu.make_async_copy(middle.at[s], gathered.at[s, :, c // ZS, c % ZS], r_sem.at[s]).start()
 
@@ -289,13 +296,18 @@
     def share_rows(s):
         landed(row_factor.at[s, :, pl.ds(0, YS - 1), core], m_sem.at[s, 3])
         rows_copy(s).start()
+
+    def ring_slice(s, q, shard):
+        if s in SHARED:
+            return gathered.at[s, q, x_lo, shard]
+        return gathered.at[s, q, :, shard]
 
     def ring_copy(s, q, k, way):
         if way == 0:
             shard, where = slot_at((z + ZS - (k - 1)) % ZS), right
         else:
             shard, where = slot_at((z + (k - 1)) % ZS), left
-        ref = gathered.at[s, q, :, shard]
+        ref = ring_slice(s, q, shard)
         return remote(ref, ref, ring_send.at[s, q, way, k - 1], ring_recv.at[s, q, way, k - 1], where)
 
     def ring_landed(s, q, k, way):
@@ -303,17 +315,28 @@
             shard = slot_at((z + ZS - k) % ZS)
         else:
             shard = slot_at((z + k) % ZS)
-        landed(gathered.at[s, q, :, shard], ring_recv.at[s, q, way, k - 1])
+        landed(ring_slice(s, q, shard), ring_recv.at[s, q, way, k - 1])
+
+    def share_slice(s, at):
+        ref = gathered.at[s, :, x_lo, slot_at(at % ZS)]
+        remote(ref, ref, x_sem.at[0, s], x_sem.at[1, s], ((1 - x_lo) * ZS + z, c)).start()
 
     def ring(s, k):
         if k == 1:
-            landed(gathered.at[s, :, :, slot_at(z)], r_sem.at[s])
+            here = gathered.at[s, :, :, slot_at(z)]
+            if s in SHARED:
+                here = gathered.at[s, :, x_lo, slot_at(z)]
+            landed(here, r_sem.at[s])
         for q in range(2):
             for way in range(2):
                 if 1 < k < 5 or (k == 5 and way == q):
                     ring_landed(s, q, k - 1, way)
                 if k < 4 or (k == 4 and way == q):
                     ring_copy(s, q, k, way).start()
+        if s in SHARED:
+            share_slice(s, z + k - 1)
+            if 1 < k < 5:
+                share_slice(s, z + ZS - (k - 1))
 
     def separate(s, m):
         if m == 0:
@@ -335,6 +358,8 @@
     def products(s):
         if s < FIRST:
             landed(gathered.at[0], r_sem.at[0])
+        if s in SHARED:
+            landed(gathered.at[s, :, 1 - x_lo], x_sem.at[1, s])
         if s == 0:
             mask_load.wait()
         keep = [
@@ -529,11 +554,21 @@
             def _():
                 first_hop(s).wait_send()
 
-            @pl.when(c != target)
-            def _():
-                second_hop(s, 0).wait_send()
-
-            second_hop(s, 1).wait_send()
+            if s in SHARED:
+                landed(gathered.at[s, :, x_lo], x_sem.at[0, s])
+
+                @pl.when(jnp.logical_not(jnp.logical_and(c == target, x_hi == x_lo)))
+                def _():
+                    second_hop(s, 0).wait_send()
+
+            else:
+
+                @pl.when(c != target)
+                def _():
+                    second_hop(s, 0).wait_send()
+
+                second_hop(s, 1).wait_send()
+
             for q in range(2):
                 for k in range(1, 5):
                     for way in range(2):
@@ -601,6 +636,7 @@
             dma((NODES, 2)),
             dma((NODES, 2)),
             dma((NODES,)),
+            dma((2, NODES)),
             dma((2, 2, 4)),
             dma((ZS, 2)),
             dma((NODES, 6)),

time: 105 us -> 102 us (0.971)
  Pallas kernels: 99.7 us -> 96.3 us
    pallas_call x1, Pallas kernels: 99.7 us -> 96.3 us  [shards(): pl.pallas_call(kernel, out_shape=(jax.ShapeDtypeStruct((NODES, 2, PIECE,...]
where the time goes in v3:
time: 102 us
  Pallas kernels  96.3 us (94%)
  local copies, waits for them, and re-layouts  2.47 us (2%)
  other arithmetic  2.41 us (2%)
    pallas_call x1, Pallas kernels, shards(): pl.pallas_call(kernel, out_shape=(jax.ShapeDtypeStruct((NODES, 2, PIECE,...  96.3 us
    unnamed x7, local copies, waits for them, and re-layouts  2.47 us
    sub x1, other arithmetic, shards(): return (inverse_cols, diag_inverse - term)  2.41 us

profile of v3, /device:TPU:1, one launch (start us, length us, event | category | flops | bytes accessed | tf_op | source)
XLA Modules:
  0.0 101.8 jit_solution(17165704728930869629)
XLA Ops:
  0.6 0.0 copy-start
  0.6 0.9 copy-done
  1.6 0.0 copy-start.1
  1.6 0.8 copy-done.1
  2.4 0.0 copy-start.2
  2.4 96.3 %shard_map.59 = (f32[3,2,32,512]{3,2,1,0:T(8,128)S(1)}, f32[3,512,512]{2,1,0:T(8,128)S(1)}) custom-call(bf16[3,2,512,2,512]{4,3,2,1,0:T(2,128)(2,1)} %bitcast.7, bf16[3,2,32,512]{3,2,1,0:T(8,128)(2,1)S(1)} %bitcast.6, s32[3,32,32]{2,1,0:T(8,128)S(1)} %copy-done.1), custom_call_target="tpu_custom_call" | custom-call | flops 3221225472 | bytes 16777216 | tf_op jit(solution)/shard_map/pallas_call | solution.py:597
  98.7 0.0 copy-done.2
  98.7 2.4 %sub.3 = f32[3,512,512]{2,1,0:T(8,128)} subtract(f32[3,512,512]{2,1,0:T(8,128)S(1)} %copy-done.2, f32[3,512,512]{2,1,0:T(8,128)S(1)} %get-tuple-element.5) | non-fusion elementwise | flops 786432 | bytes 9437184 | tf_op jit(solution)/shard_map/sub | solution.py:664
  101.1 0.7 copy.8
Async XLA Ops:
  0.6 0.9 copy-start
  1.6 0.8 copy-start.1
  2.4 96.3 %copy-start.2 = (f32[3,512,512]{2,1,0:T(8,128)S(1)}, f32[3,512,512]{2,1,0:T(8,128)}, u32[]{:S(2)}) copy-start(f32[3,512,512]{2,1,0:T(8,128)} %param.6) | copy-start | bytes 9437188

commit v4 on v3

--- a/solution.py
+++ b/solution.py
@@ -529,7 +529,7 @@
     order = (
         "B0", "B1", "B2", "D00", "D01", "P0", "A0", "D10", "P1", "D11", "R01", "A1",
         "P2", "D20", "R02", "R11", "D21", "R03", "R12", "A2", "F0", "R04", "R13", "F1",
-        "R05", "R14", "10", "R21", "40", "F2", "R15", "R22", "20", "50", "11", "R23",
+        "R21", "R05", "R14", "10", "R22", "40", "F2", "R15", "R23", "20", "50", "11",
         "R24", "21", "41", "51", "60", "R25", "12", "42", "52", "70", "61", "30",
         "62", "22", "80", "71", "72", "31", "81", "90", "82", "91", "32", "92",
     )

time: 102 us -> 103 us (level); the launches traced: 102 us -> 102 us
  no operation moved by 1% of the time
where the time goes in v4:
time: 103 us; the launch traced here: 102 us
  Pallas kernels  96.1 us (93%)
  local copies, waits for them, and re-layouts  2.47 us (2%)
  other arithmetic  2.41 us (2%)
    pallas_call x1, Pallas kernels, shards(): pl.pallas_call(kernel, out_shape=(jax.ShapeDtypeStruct((NODES, 2, PIECE,...  96.1 us
    unnamed x7, local copies, waits for them, and re-layouts  2.47 us
    sub x1, other arithmetic, shards(): return (inverse_cols, diag_inverse - term)  2.41 us

profile of v4, /device:TPU:1, one launch (start us, length us, event | category | flops | bytes accessed | tf_op | source)
XLA Modules:
  0.0 101.7 jit_solution(13054528119626469862)
XLA Ops:
  0.6 0.0 copy-start
  0.6 0.9 copy-done
  1.6 0.0 copy-start.1
  1.6 0.8 copy-done.1
  2.4 0.0 copy-start.2
  2.4 96.1 %shard_map.59 = (f32[3,2,32,512]{3,2,1,0:T(8,128)S(1)}, f32[3,512,512]{2,1,0:T(8,128)S(1)}) custom-call(bf16[3,2,512,2,512]{4,3,2,1,0:T(2,128)(2,1)} %bitcast.7, bf16[3,2,32,512]{3,2,1,0:T(8,128)(2,1)S(1)} %bitcast.6, s32[3,32,32]{2,1,0:T(8,128)S(1)} %copy-done.1), custom_call_target="tpu_custom_call" | custom-call | flops 3221225472 | bytes 16777216 | tf_op jit(solution)/shard_map/pallas_call | solution.py:597
  98.5 0.0 copy-done.2
  98.5 2.4 %sub.3 = f32[3,512,512]{2,1,0:T(8,128)} subtract(f32[3,512,512]{2,1,0:T(8,128)S(1)} %copy-done.2, f32[3,512,512]{2,1,0:T(8,128)S(1)} %get-tuple-element.5) | non-fusion elementwise | flops 786432 | bytes 9437184 | tf_op jit(solution)/shard_map/sub | solution.py:664
  100.9 0.7 copy.8
Async XLA Ops:
  0.6 0.9 copy-start
  1.6 0.8 copy-start.1
  2.4 96.2 %copy-start.2 = (f32[3,512,512]{2,1,0:T(8,128)S(1)}, f32[3,512,512]{2,1,0:T(8,128)}, u32[]{:S(2)}) copy-start(f32[3,512,512]{2,1,0:T(8,128)} %param.6) | copy-start | bytes 9437188
